TPU v7x, 32 devices: a whole 2x2x4 slice. The times are simulated.
32 devices in a mesh: replica: 2 (over y), gx: 8 (over z, x), gy: 2 (over core).
Axes of the slice: x: 2, y: 2, z: 4, core: 2. Of those that a mesh axis runs over, the one named last changes fastest.
Arguments:
- hidden: bfloat16 [16, 8192], P(('replica', 'gx')), parts along dimension 0, may hold values from -6 to 6
- exit_layer: int32 [2], P('replica'), parts along dimension 0, may hold values from 0 to 79
- norm_gains: bfloat16 [80, 8192], P(None, 'gx'), may hold values from 0.099609375 to 1.8984375
- w_query: bfloat16 [8192, 8192], P('gx', 'gy'), may hold values from -0.0625 to 0.0625
- key_weight: bfloat16 [8192, 1024], P('gx', 'gy'), may hold values from -0.0625 to 0.0625
- value_weight: bfloat16 [8192, 1024], P('gx', 'gy'), may hold values from -0.0625 to 0.0625
- w_out: bfloat16 [8192, 8192], P('gy', 'gx'), may hold values from -0.0625 to 0.0625
- key_cache: bfloat16 [16, 8, 512, 128], P(('replica', 'gx'), 'gy'), parts along dimension 0
- cached_value_rows: bfloat16 [16, 8, 512, 128], P(('replica', 'gx'), 'gy'), parts along dimension 0, may hold values from -6 to 6
- lengths: int32 [16], P(('replica', 'gx')), parts along dimension 0, may hold values from 1 to 512, as said below
Outputs:
- layer_out: bfloat16 [16, 8192], P('replica', 'gx'), parts along dimension 0
There are 2 independent parts, one for each index of `replica`. A program takes and returns all parts, laid end to end along the dimension named above; an argument that names none is the same for every part. Nothing has to cross between parts.
Inputs may be any that keep to these rules, and one draw needn't show every extreme that they name: Slots 0 to lengths[r] - 1 of row r are filled; the new token sits at position lengths[r].
All inputs are finite; a program needn't handle non-finite values.
Results may differ from a plain program's by a relative error of at most 0.012.
The roundings to bfloat16 on the way count: a program that leaves them out, or rounds other values in their place, can miss the bound.
Values may be sent and summed in bfloat16 or wider, within the bound.
A program may use at most 64 MiB of HBM per device.

v0:
```python
import math

import jax
import jax.numpy as jnp
from jax import lax
from jax.sharding import PartitionSpec as P


def rotate(vectors, positions):
    half = vectors.shape[-1] // 2
    steps = jnp.arange(half, dtype=jnp.float32) * (2.0 / vectors.shape[-1])
    freqs = jnp.exp(-math.log(500000.0) * steps)
    angles = positions[:, None, None] * freqs[None, None, :]
    cosine = jnp.cos(angles)
    sine = jnp.sin(angles)
    first = vectors[..., :half]
    second = vectors[..., half:]
    return jnp.concatenate(
        [first * cosine - second * sine, second * cosine + first * sine], axis=-1
    )


def body(
    hidden,
    exit_layer,
    norm_gains,
    w_query,
    key_weight,
    value_weight,
    w_out,
    key_cache,
    cached_value_rows,
    lengths,
):
    rows_dev = hidden.shape[0]
    head = key_cache.shape[3]
    kv_local = key_cache.shape[1]
    q_local = w_query.shape[1] // head
    group = q_local // kv_local
    columns = lax.all_to_all(hidden, "gx", split_axis=1, concat_axis=0, tiled=True)
    x32 = columns.astype(jnp.float32)
    own_rows = hidden.astype(jnp.float32)
    inv_local = lax.rsqrt(jnp.mean(own_rows * own_rows, axis=-1) + 1e-05)
    inv = lax.all_gather(inv_local, "gx", axis=0, tiled=True)
    gain = lax.dynamic_index_in_dim(norm_gains, exit_layer[0], 0, keepdims=False).astype(
        jnp.float32
    )
    normed = (x32 * inv[:, None] * gain[None, :]).astype(jnp.bfloat16)
    weights = jnp.concatenate([w_query, key_weight, value_weight], axis=1)
    width_q = w_query.shape[1]
    width_k = key_weight.shape[1]
    partial_sums = jnp.dot(normed, weights, preferred_element_type=jnp.float32)
    shares = lax.psum_scatter(partial_sums, "gx", scatter_dimension=1, tiled=True)
    projected = lax.all_to_all(shares, "gx", split_axis=0, concat_axis=1, tiled=True)
    query = projected[:, :width_q]
    keys = projected[:, width_q : width_q + width_k]
    values = projected[:, width_q + width_k :]
    positions = lengths.astype(jnp.float32)
    rq = rotate(query.reshape(rows_dev, q_local, head), positions).astype(jnp.bfloat16)
    rk = rotate(keys.reshape(rows_dev, kv_local, head), positions).astype(jnp.bfloat16)
    nv = values.reshape(rows_dev, kv_local, head).astype(jnp.bfloat16)
    scale = 1.0 / math.sqrt(head)
    grouped = rq.reshape(rows_dev, kv_local, group, head)
    scores = (
        jnp.einsum("rgqd,rgpd->rgqp", grouped, key_cache, preferred_element_type=jnp.float32)
        * scale
    )
    own = jnp.einsum("rgqd,rgd->rgq", grouped, rk, preferred_element_type=jnp.float32) * scale
    valid = jnp.arange(key_cache.shape[2], dtype=jnp.int32)[None, :] < lengths[:, None]
    scores = jnp.where(valid[:, None, None, :], scores, -1e30)
    top = jnp.maximum(jnp.max(scores, axis=-1), own)
    weights_exp = jnp.where(valid[:, None, None, :], jnp.exp(scores - top[..., None]), 0.0)
    own_weight = jnp.exp(own - top)
    total = jnp.sum(weights_exp, axis=-1) + own_weight
    probs = (weights_exp / total[..., None]).astype(jnp.bfloat16)
    own_prob = (own_weight / total).astype(jnp.bfloat16)
    attn = jnp.einsum(
        "rgqp,rgpd->rgqd", probs, cached_value_rows, preferred_element_type=jnp.float32
    )
    attn = attn + own_prob.astype(jnp.float32)[..., None] * nv.astype(jnp.float32)[:, :, None, :]
    attn = attn.reshape(rows_dev, q_local * head).astype(jnp.bfloat16)
    mixed = jnp.dot(
        lax.all_gather(attn, "gx", axis=0, tiled=True), w_out, preferred_element_type=jnp.float32
    )
    summed = lax.psum(mixed, "gy")
    return (x32 + summed).astype(jnp.bfloat16)


def solution(mesh):
    placed = (
        P(("replica", "gx"), None),
        P("replica"),
        P(None, "gx"),
        P("gx", "gy"),
        P("gx", "gy"),
        P("gx", "gy"),
        P("gy", "gx"),
        P(("replica", "gx"), "gy", None, None),
        P(("replica", "gx"), "gy", None, None),
        P(("replica", "gx")),
    )
    return jax.shard_map(
        body, mesh=mesh, in_specs=placed, out_specs=P("replica", "gx"), check_vma=False
    )
```

profile of v0, /device:TPU:0, one launch (start us, length us, event | category | flops | bytes accessed | tf_op | source)
XLA Modules:
  0.0 159.9 jit_solution(2081836546267267508)
XLA Ops:
  6.5 0.0 copy-start
  6.5 0.5 broadcast.50
  7.0 1.5 reduce.5
  8.5 0.6 reshape.194
  9.2 7.3 %all-to-all-start = ((bf16[8,2,512]{2,1,0:T(2,128)(2,1)}), bf16[8,2,512]{2,1,0:T(2,128)(2,1)S(1)}, u32[]{:S(2)}, u32[]{:S(2)}) async-start(bf16[8,2,512]{2,1,0:T(2,128)(2,1)} %reshape.194), calls=%async_computation | async-start | bytes 32768 | tf_op jit(solution)/shard_map/all_to_all | solution.py:40
  16.4 0.0 reduce-scatter.2.cloned.1.call-start
  16.5 1.4 multiply_reduce_fusion
  19.2 1.3 dynamic-slice
  20.4 0.7 dynamic-update-slice
  21.2 0.7 dynamic-slice_convert_fusion
  21.9 21.8 %all-reduce = f32[8]{0:T(128)S(1)} all-reduce(f32[8]{0:T(128)S(1)} %dynamic-update-slice), channel_id=1, replica_groups=mesh['replica'=2,'gx'=8,'gy'=2] {'gx'}, use_global_device_ids=true, to_apply=%add | all-reduce | flops 8 | bytes 64
  43.7 0.0 all-to-all-done
  43.7 0.0 copy-start.1
  43.7 5.6 %fusion = f32[8,5120]{1,0:T(8,128)} fusion(bf16[1024,512]{1,0:T(8,128)(2,1)} %param.15, bf16[1024,512]{1,0:T(8,128)(2,1)} %param.14, bf16[1024,4096]{1,0:T(8,128)(2,1)} %param.13, f32[1024]{0:T(1024)S(1)} %bitcast.60, f32[8]{0:T(128)S(1)} %all-reduce, bf16[1,8,1024]{2,0,1:T(2,128)(2,1)S(1)} %bitcast.51), kind=kOutput, calls=%fused_computation | convolution fusion | flops 115376128 | bytes 10670112 | tf_op jit(solution)/shard_map/dot_general | solution.py:52
  49.3 0.0 reduce-scatter.2.cloned.1.call-update
  50.1 51.0 %reduce-scatter.2.cloned.1.call-done = f32[8,640]{1,0:T(8,128)} async-done(((f32[8,5120]{1,0:T(8,128)}), f32[8,640]{1,0:T(8,128)}) %reduce-scatter.2.cloned.1.call-update) | async-done | bytes 20496 | tf_op jit(solution)/shard_map/reduce_scatter | solution.py:53
  101.1 1.3 copy.13
  102.4 3.7 %all-to-all-start.1 = ((f32[8,1,640]{2,1,0:T(1,128)}), f32[8,1,640]{2,1,0:T(1,128)S(1)}, u32[]{:S(2)}, u32[]{:S(2)}) async-start(f32[8,1,640]{2,1,0:T(1,128)} %copy.13), calls=%async_computation.2 | async-start | bytes 40960 | tf_op jit(solution)/shard_map/all_to_all | solution.py:54
  106.1 6.6 %all-to-all-done.1 = f32[8,1,640]{2,1,0:T(1,128)S(1)} async-done(((f32[8,1,640]{2,1,0:T(1,128)}), f32[8,1,640]{2,1,0:T(1,128)S(1)}, u32[]{:S(2)}, u32[]{:S(2)}) %all-to-all-start.1) | async-done | bytes 20512 | tf_op jit(solution)/shard_map/all_to_all | solution.py:54
  112.7 0.1 fusion.31
  112.8 0.1 fusion.25
  112.8 0.1 maximum_bitcast_fusion
  112.9 0.2 fusion.29
  113.1 0.0 copy-done
  113.1 0.4 fusion.41
  113.5 0.2 fusion.13
  113.7 0.0 copy-done.1
  113.7 0.2 fusion.7
  114.0 30.5 %all-gather = bf16[8,1,4096]{2,1,0:T(2,128)(2,1)S(1)} all-gather(bf16[1,1,4096]{2,1,0:T(2,128)(2,1)S(1)} %reshape.187), channel_id=1, replica_groups=mesh['replica'=2,'gx'=8,'gy'=2] {'gx'}, dimensions={0}, use_global_device_ids=true | all-gather | bytes 73728 | tf_op jit(solution)/shard_map/all_gather | solution.py:83
  144.5 4.6 %fusion.10 = f32[8,1024]{1,0:T(8,128)S(1)} fusion(bf16[4096,1024]{1,0:T(8,128)(2,1)} %param.16, bf16[8,1,4096]{2,1,0:T(2,128)(2,1)S(1)} %all-gather), kind=kOutput, calls=%fused_computation.12 | convolution fusion | flops 67108864 | bytes 8486912 | tf_op jit(solution)/shard_map/dot_general | solution.py:82
  149.1 3.4 %psum.7 = f32[8,1024]{1,0:T(8,128)S(1)} all-reduce(f32[8,1024]{1,0:T(8,128)S(1)} %fusion.10), channel_id=1, replica_groups=mesh['replica'=2,'gx'=8,'gy'=2] {'gy'}, use_global_device_ids=true, to_apply=%region_4.5 | all-reduce | flops 8192 | bytes 65536 | tf_op jit(solution)/shard_map/psum | solution.py:85
  152.5 0.6 fusion.16
  (10 shorter events, 0.1 us)
Async XLA Ops:
  6.5 106.6 %copy-start = (bf16[1,4,512,128]{3,2,1,0:T(8,128)(2,1)S(1)}, bf16[1,4,512,128]{3,2,1,0:T(8,128)(2,1)}, u32[]{:S(2)}) copy-start(bf16[1,4,512,128]{3,2,1,0:T(8,128)(2,1)} %param.17) | copy-start | bytes 1572868
  9.2 34.5 %all-to-all-start = ((bf16[8,2,512]{2,1,0:T(2,128)(2,1)}), bf16[8,2,512]{2,1,0:T(2,128)(2,1)S(1)}, u32[]{:S(2)}, u32[]{:S(2)}) async-start(bf16[8,2,512]{2,1,0:T(2,128)(2,1)} %reshape.194), calls=%async_computation | async-start | bytes 32768 | tf_op jit(solution)/shard_map/all_to_all | solution.py:40
  16.4 84.7 %reduce-scatter.2.cloned.1.call-start = ((), (), s32[]{:S(2)}) async-start(), calls=%async_computation.3 | async-start | bytes 184320 | tf_op jit(solution)/shard_map/reduce_scatter | solution.py:53
  43.7 70.0 %copy-start.1 = (bf16[1,4,512,128]{3,2,1,0:T(8,128)(2,1)S(1)}, bf16[1,4,512,128]{3,2,1,0:T(8,128)(2,1)}, u32[]{:S(2)}) copy-start(bf16[1,4,512,128]{3,2,1,0:T(8,128)(2,1)} %param.18) | copy-start | bytes 1572868
  102.4 10.3 %all-to-all-start.1 = ((f32[8,1,640]{2,1,0:T(1,128)}), f32[8,1,640]{2,1,0:T(1,128)S(1)}, u32[]{:S(2)}, u32[]{:S(2)}) async-start(f32[8,1,640]{2,1,0:T(1,128)} %copy.13), calls=%async_computation.2 | async-start | bytes 40960 | tf_op jit(solution)/shard_map/all_to_all | solution.py:54
Sparse Core Ops, SparseCore 0:
  49.5 51.5 reduce-scatter.1
where the time goes:
time: 161 us; the launch traced here: 160 us
  waiting for transfers between devices  57.6 us (36%)
  blocking collectives  55.7 us (35%)
  between operations  15.4 us (10%)
  matrix products  11 us (7%)
  starting transfers between devices  10.9 us (7%)
  other arithmetic  4.76 us (3%)
  local copies, waits for them, and re-layouts  4.53 us (3%)
    reduce_scatter x1, waiting for transfers between devices, body(): lax.psum_scatter(partial_sums, 'gx', scatter_dimension=1, tiled=True)  51 us
    all_gather x1, blocking collectives, body(): lax.all_gather(attn, 'gx', axis=0, tiled=True)  30.5 us
    unnamed x1, blocking collectives  21.8 us
    all_to_all x1, starting transfers between devices, body(): lax.all_to_all(hidden, 'gx', split_axis=1, concat_axis=0, tiled=True)  7.25 us
    all_to_all x1, waiting for transfers between devices, body(): lax.all_to_all(shares, 'gx', split_axis=0, concat_axis=1, tiled=True)  6.6 us
    dot_general x1, matrix products, body(): partial_sums = jnp.dot(normed, weights, preferred_element_type=jnp.float32)  5.63 us
    dot_general x1, matrix products, body(): jnp.dot(lax.all_gather(attn, 'gx', axis=0, tiled=True), w_out, preferred_...  4.59 us
    all_to_all x1, starting transfers between devices, body(): lax.all_to_all(shares, 'gx', split_axis=0, concat_axis=1, tiled=True)  3.65 us
  transfers between devices with their start and end apart: 3, of which 2 were waited for; matrix products, arithmetic and copies ran while one was open for 3% of the time, Pallas kernels for 0%

commit v1 on v0

--- a/solution.py
+++ b/solution.py
@@ -1,9 +1,284 @@
+import functools
 import math
 
 import jax
 import jax.numpy as jnp
 from jax import lax
+from jax.experimental import pallas as pl
+from jax.experimental.pallas import tpu as pltpu
 from jax.sharding import PartitionSpec as P
+
+MESH = pl.DeviceIdType.MESH
+LANES = 128
+QUERY_PIECES = 4
+OUT_PIECES = 2
+
+
+def kernel(
+    gx,
+    hidden_ref,
+    layer_ref,
+    length_ref,
+    gains_hbm,
+    wq_hbm,
+    wk_hbm,
+    wv_hbm,
+    wo_hbm,
+    kc_hbm,
+    vc_hbm,
+    out_ref,
+    gains_ref,
+    wq_ref,
+    wk_ref,
+    wv_ref,
+    wo_ref,
+    kc_ref,
+    vc_ref,
+    x_send,
+    x_recv,
+    p_send,
+    p_recv,
+    a_send,
+    a_recv,
+    y_send,
+    y_recv,
+    local_sems,
+    x_sems,
+    p_sems,
+    a_sems,
+    y_sems,
+):
+    me = lax.axis_index("gx")
+    core = lax.axis_index("gy")
+    other = 1 - core
+    peers = [lax.rem(me + d, gx) for d in range(1, gx)]
+    cols = x_recv.shape[2] - LANES
+    kv_local, slots, head = kc_ref.shape
+    q_local = wq_ref.shape[1] // head
+    group = q_local // kv_local
+
+    barrier = pltpu.get_barrier_semaphore()
+    for peer in peers:
+        pl.semaphore_signal(barrier, inc=1, device_id={"gx": peer}, device_id_type=MESH)
+    pl.semaphore_signal(barrier, inc=1, device_id={"gy": other}, device_id_type=MESH)
+
+    width = wq_ref.shape[1] // QUERY_PIECES
+    pairs = [(gains_hbm, gains_ref)]
+    for i in range(QUERY_PIECES):
+        piece = pl.ds(i * width, width)
+        pairs.append((wq_hbm.at[:, piece], wq_ref.at[:, piece]))
+    pairs += [(wk_hbm, wk_ref), (wv_hbm, wv_ref), (kc_hbm.at[0], kc_ref), (vc_hbm.at[0], vc_ref)]
+    out_width = wo_ref.shape[1] // OUT_PIECES
+    for i in range(OUT_PIECES):
+        piece = pl.ds(i * out_width, out_width)
+        pairs.append((wo_hbm.at[:, piece], wo_ref.at[:, piece]))
+    loads = [
+        pltpu.make_async_copy(src, dst, local_sems.at[i]) for i, (src, dst) in enumerate(pairs)
+    ]
+    for load in loads:
+        load.start()
+
+    def exchange(src, dst, sems):
+        copies = [
+            pltpu.make_async_remote_copy(
+                src_ref=src(peer),
+                dst_ref=dst.at[me],
+                send_sem=sems.at[0, peer],
+                recv_sem=sems.at[1, me],
+                device_id={"gx": peer},
+                device_id_type=MESH,
+            )
+            for peer in peers
+        ]
+        for copy in copies:
+            copy.start()
+        return copies
+
+    def arrive(src, dst, sems):
+        for peer in peers:
+            pltpu.make_async_remote_copy(
+                src_ref=src(peer),
+                dst_ref=dst.at[peer],
+                send_sem=sems.at[0, peer],
+                recv_sem=sems.at[1, peer],
+                device_id={"gx": peer},
+                device_id_type=MESH,
+            ).wait_recv()
+
+    row = hidden_ref[...].astype(jnp.float32)
+    inv_row = lax.rsqrt(jnp.mean(row * row, axis=-1, keepdims=True) + 1e-05)
+    inv_lanes = jnp.broadcast_to(inv_row, (1, LANES))
+    for j in range(gx):
+        x_send[j, :, :cols] = row[:, j * cols : (j + 1) * cols]
+        x_send[j, :, cols:] = inv_lanes
+    x_recv[me] = x_send[me]
+    pl.semaphore_wait(barrier, gx)
+    x_copies = exchange(lambda peer: x_send.at[peer], x_recv, x_sems)
+
+    half = head // 2
+    lane = lax.broadcasted_iota(jnp.int32, (1, head), 1)
+    index = jnp.where(lane < half, lane, lane - half).astype(jnp.float32)
+    freqs = jnp.exp(-math.log(500000.0) * (index * (2.0 / head)))
+    length = length_ref[0]
+    angles = length.astype(jnp.float32) * freqs
+    cosine = jnp.cos(angles)
+    sine = jnp.sin(angles)
+    sine = jnp.where(lane < half, -sine, sine)
+
+    loads[0].wait()
+    table = gains_ref[...].astype(jnp.float32)
+    chosen = lax.broadcasted_iota(jnp.int32, table.shape, 0) == layer_ref[0]
+    gain = jnp.sum(jnp.where(chosen, table, 0.0), axis=0, keepdims=True)
+
+    arrive(lambda peer: x_send.at[peer], x_recv, x_sems)
+    x32 = x_recv[:, 0, :cols]
+    inv = x_recv[:, 0, cols : cols + 1]
+    normed = (x32 * inv * gain).astype(jnp.bfloat16)
+
+    def project(weights, first):
+        sums = jnp.dot(normed, weights, preferred_element_type=jnp.float32)
+        for h in range(sums.shape[1] // head):
+            p_send[:, first + h, :] = sums[:, h * head : (h + 1) * head]
+
+    for i in range(QUERY_PIECES):
+        loads[1 + i].wait()
+        project(wq_ref[:, i * width : (i + 1) * width], i * width // head)
+    loads[1 + QUERY_PIECES].wait()
+    project(wk_ref[...], q_local)
+    loads[2 + QUERY_PIECES].wait()
+    project(wv_ref[...], q_local + kv_local)
+    p_copies = exchange(lambda peer: p_send.at[peer], p_recv, p_sems)
+    p_recv[me] = p_send[me]
+    loads[3 + QUERY_PIECES].wait()
+    loads[4 + QUERY_PIECES].wait()
+    arrive(lambda peer: p_send.at[peer], p_recv, p_sems)
+    total = p_recv[0]
+    for j in range(1, gx):
+        total = total + p_recv[j]
+
+    rotated = total * cosine + pltpu.roll(total, half, 1) * sine
+    scale = 1.0 / math.sqrt(head)
+    valid = lax.broadcasted_iota(jnp.int32, (1, slots), 1) < length
+    for g in range(kv_local):
+        rq = rotated[g * group : (g + 1) * group].astype(jnp.bfloat16)
+        rk = rotated[q_local + g : q_local + g + 1].astype(jnp.bfloat16).astype(jnp.float32)
+        first = q_local + kv_local + g
+        nv = total[first : first + 1].astype(jnp.bfloat16).astype(jnp.float32)
+        scores = (
+            lax.dot_general(
+                rq, kc_ref[g], (((1,), (1,)), ((), ())), preferred_element_type=jnp.float32
+            )
+            * scale
+        )
+        own = jnp.sum(rq.astype(jnp.float32) * rk, axis=-1, keepdims=True) * scale
+        scores = jnp.where(valid, scores, -1e30)
+        top = jnp.maximum(jnp.max(scores, axis=-1, keepdims=True), own)
+        exps = jnp.where(valid, jnp.exp(scores - top), 0.0)
+        own_exp = jnp.exp(own - top)
+        denominator = jnp.sum(exps, axis=-1, keepdims=True) + own_exp
+        probs = (exps / denominator).astype(jnp.bfloat16)
+        own_prob = (own_exp / denominator).astype(jnp.bfloat16).astype(jnp.float32)
+        attn = jnp.dot(probs, vc_ref[g], preferred_element_type=jnp.float32) + own_prob * nv
+        a_send[g * group : (g + 1) * group, :] = attn.astype(jnp.bfloat16).astype(jnp.float32)
+    a_copies = exchange(lambda peer: a_send, a_recv, a_sems)
+    a_recv[me] = a_send[...]
+    for i in range(OUT_PIECES):
+        loads[5 + QUERY_PIECES + i].wait()
+    arrive(lambda peer: a_send, a_recv, a_sems)
+    attended = jnp.concatenate([a_recv[:, h, :] for h in range(q_local)], axis=1).astype(
+        jnp.bfloat16
+    )
+    y_copies = []
+    for i in range(OUT_PIECES):
+        piece = slice(i * out_width, (i + 1) * out_width)
+        y_send[i] = jnp.dot(attended, wo_ref[:, piece], preferred_element_type=jnp.float32)
+        copy = pltpu.make_async_remote_copy(
+            src_ref=y_send.at[i],
+            dst_ref=y_recv.at[i],
+            send_sem=y_sems.at[0, i],
+            recv_sem=y_sems.at[1, i],
+            device_id={"gy": other},
+            device_id_type=MESH,
+        )
+        copy.start()
+        y_copies.append(copy)
+    for i in range(OUT_PIECES):
+        y_copies[i].wait_recv()
+        piece = slice(i * out_width, (i + 1) * out_width)
+        summed = y_send[i] + y_recv[i]
+        out_ref[:, piece] = (x_recv[:, 0, piece] + summed).astype(out_ref.dtype)
+    for copy in x_copies + p_copies + a_copies + y_copies:
+        copy.wait_send()
+
+
+def fused(
+    hidden,
+    exit_layer,
+    norm_gains,
+    w_query,
+    key_weight,
+    value_weight,
+    w_out,
+    key_cache,
+    cached_value_rows,
+    lengths,
+):
+    gx = lax.axis_size("gx")
+    cols = norm_gains.shape[1]
+    _, kv_local, slots, head = key_cache.shape
+    q_local = w_query.shape[1] // head
+    heads = q_local + 2 * kv_local
+    f32, bf16 = jnp.float32, jnp.bfloat16
+    vmem = pl.BlockSpec(memory_space=pltpu.VMEM)
+    smem = pl.BlockSpec(memory_space=pltpu.SMEM)
+    anywhere = pl.BlockSpec(memory_space=pl.ANY)
+    dma = pltpu.SemaphoreType.DMA
+    weights = w_query.size + key_weight.size + value_weight.size + w_out.size
+    return pl.pallas_call(
+        functools.partial(kernel, gx),
+        out_shape=jax.ShapeDtypeStruct((gx, cols), bf16),
+        in_specs=[vmem, smem, smem] + [anywhere] * 7,
+        out_specs=vmem,
+        scratch_shapes=[
+            pltpu.VMEM(norm_gains.shape, bf16),
+            pltpu.VMEM(w_query.shape, bf16),
+            pltpu.VMEM(key_weight.shape, bf16),
+            pltpu.VMEM(value_weight.shape, bf16),
+            pltpu.VMEM(w_out.shape, bf16),
+            pltpu.VMEM(key_cache.shape[1:], bf16),
+            pltpu.VMEM(key_cache.shape[1:], bf16),
+            pltpu.VMEM((gx, 1, cols + LANES), f32),
+            pltpu.VMEM((gx, 1, cols + LANES), f32),
+            pltpu.VMEM((gx, heads, head), f32),
+            pltpu.VMEM((gx, heads, head), f32),
+            pltpu.VMEM((q_local, head), f32),
+            pltpu.VMEM((gx, q_local, head), f32),
+            pltpu.VMEM((OUT_PIECES, gx, cols // OUT_PIECES), f32),
+            pltpu.VMEM((OUT_PIECES, gx, cols // OUT_PIECES), f32),
+            dma((5 + QUERY_PIECES + OUT_PIECES,)),
+            dma((2, gx)),
+            dma((2, gx)),
+            dma((2, gx)),
+            dma((2, OUT_PIECES)),
+        ],
+        compiler_params=pltpu.CompilerParams(
+            collective_id=0, has_side_effects=True, vmem_limit_bytes=56 * 2**20
+        ),
+        cost_estimate=pl.CostEstimate(
+            flops=2 * gx * weights, bytes_accessed=2 * weights, transcendentals=0
+        ),
+    )(
+        hidden,
+        exit_layer,
+        lengths,
+        norm_gains,
+        w_query,
+        key_weight,
+        value_weight,
+        w_out,
+        key_cache,
+        cached_value_rows,
+    )
 
 
 def rotate(vectors, positions):
@@ -86,6 +361,13 @@
     return (x32 + summed).astype(jnp.bfloat16)
 
 
+def step(*arrays):
+    hidden, gains = arrays[0], arrays[2]
+    if gains.shape[1] % (LANES * OUT_PIECES) == 0 and hidden.shape[0] == 1:
+        return fused(*arrays)
+    return body(*arrays)
+
+
 def solution(mesh):
     placed = (
         P(("replica", "gx"), None),
@@ -100,5 +382,5 @@
         P(("replica", "gx")),
     )
     return jax.shard_map(
-        body, mesh=mesh, in_specs=placed, out_specs=P("replica", "gx"), check_vma=False
-    )
+        step, mesh=mesh, in_specs=placed, out_specs=P("replica", "gx"), check_vma=False
+    )

time: 161 us -> 28.7 us (0.18)
  waiting for transfers between devices: 57.6 us -> 0 us
  blocking collectives: 55.7 us -> 0 us
  Pallas kernels: 0 us -> 25.8 us
  between operations: 15.4 us -> 1.3 us
  matrix products: 11 us -> 0 us
  starting transfers between devices: 10.9 us -> 0 us
  other arithmetic: 4.76 us -> 0 us
  local copies, waits for them, and re-layouts: 4.53 us -> 1.32 us
    reduce_scatter x1 -> x0, waiting for transfers between devices: 51 us -> none  [body(): lax.psum_scatter(partial_sums, 'gx', scatter_dimension=1, tiled=True)]
    all_gather x1 -> x0, blocking collectives: 30.5 us -> none  [body(): lax.all_gather(attn, 'gx', axis=0, tiled=True)]
    pallas_call x0 -> x1, Pallas kernels: none -> 25.8 us  [fused(): pl.pallas_call(functools.partial(kernel, gx), out_shape=jax.ShapeDtypeStr...]
    unnamed x1 -> x0, blocking collectives: 21.8 us -> none
    dot_general x5 -> x0, matrix products: 11 us -> none  [the longest x1 5.63 us: body(): partial_sums = jnp.dot(normed, weights, preferred_element_type=jnp.float32)]
    all_to_all x2 -> x0, starting transfers between devices: 10.9 us -> none  [the longest x1 7.25 us: body(): lax.all_to_all(hidden, 'gx', split_axis=1, concat_axis=0, tiled=True)]
    all_to_all x2 -> x0, waiting for transfers between devices: 6.6 us -> none  [the longest x1 6.6 us: body(): lax.all_to_all(shares, 'gx', split_axis=0, concat_axis=1, tiled=True)]
    psum x1 -> x0, blocking collectives: 3.4 us -> none  [body(): summed = lax.psum(mixed, 'gy')]
  transfers between devices with their start and end apart: 3 -> 0, of which waited for: 2 -> 0; matrix products, arithmetic and copies ran while one was open for 3% -> 0% of each run, Pallas kernels for 0% -> 0%
where the time goes in v1:
time: 28.7 us; the launch traced here: 28.4 us
  Pallas kernels  25.8 us (90%)
  local copies, waits for them, and re-layouts  1.32 us (5%)
  between operations  1.3 us (5%)
    pallas_call x1, Pallas kernels, fused(): pl.pallas_call(functools.partial(kernel, gx), out_shape=jax.ShapeDtypeStr...  25.8 us
    unnamed x1, local copies, waits for them, and re-layouts  1.32 us

profile of v1, /device:TPU:0, one launch (start us, length us, event | category | flops | bytes accessed | tf_op | source)
XLA Modules:
  0.0 28.4 jit_solution(10883217631905444051)
XLA Ops:
  1.3 25.8 %shard_map.100 = bf16[8,1024]{1,0:T(8,128)(2,1)} custom-call(bf16[1,8192]{1,0:T(2,128)(2,1)} %hidden_ref.1, s32[1]{0:T(128)S(6)} %copy.12.layer_ref, s32[1]{0:T(128)S(6)} %copy.13.length_ref, bf16[80,1024]{1,0:T(8,128)(2,1)} %gains_hbm.1, bf16[1024,4096]{1,0:T(8,128)(2,1)} %wq_hbm.1, bf16[1024,512]{1,0:T(8,128)(2,1)} %wk_hbm.1, bf16[1024,512]{1,0:T(8,128)(2,1)} %wv_hbm.1, ...), custom_call_target="tpu_custom_call" | custom-call | flops 150994944 | bytes 18874368 | tf_op jit(solution)/shard_map/pallas_call | solution.py:237
  27.1 1.3 %copy.14 = bf16[8,1024]{1,0:T(8,128)(2,1)} copy(bf16[8,1024]{1,0:T(8,128)(2,1)} %shard_map.100) | data formatting | bytes 32768

commit v2 on v1

--- a/solution.py
+++ b/solution.py
@@ -10,15 +10,13 @@
 
 MESH = pl.DeviceIdType.MESH
 LANES = 128
-QUERY_PIECES = 4
 OUT_PIECES = 2
 
 
 def kernel(
     gx,
     hidden_ref,
-    layer_ref,
-    length_ref,
+    ints_ref,
     gains_hbm,
     wq_hbm,
     wk_hbm,
@@ -40,6 +38,7 @@
     p_recv,
     a_send,
     a_recv,
+    a_wide,
     y_send,
     y_recv,
     local_sems,
@@ -62,48 +61,42 @@
         pl.semaphore_signal(barrier, inc=1, device_id={"gx": peer}, device_id_type=MESH)
     pl.semaphore_signal(barrier, inc=1, device_id={"gy": other}, device_id_type=MESH)
 
-    width = wq_ref.shape[1] // QUERY_PIECES
+    width = wq_ref.shape[1] // kv_local
+    depth = wo_ref.shape[0] // OUT_PIECES
     pairs = [(gains_hbm, gains_ref)]
-    for i in range(QUERY_PIECES):
+    pairs += [(wk_hbm, wk_ref), (wv_hbm, wv_ref)]
+    for i in range(kv_local):
         piece = pl.ds(i * width, width)
         pairs.append((wq_hbm.at[:, piece], wq_ref.at[:, piece]))
-    pairs += [(wk_hbm, wk_ref), (wv_hbm, wv_ref), (kc_hbm.at[0], kc_ref), (vc_hbm.at[0], vc_ref)]
-    out_width = wo_ref.shape[1] // OUT_PIECES
+    pairs += [(kc_hbm.at[0], kc_ref), (vc_hbm.at[0], vc_ref)]
     for i in range(OUT_PIECES):
-        piece = pl.ds(i * out_width, out_width)
-        pairs.append((wo_hbm.at[:, piece], wo_ref.at[:, piece]))
+        piece = pl.ds(i * depth, depth)
+        pairs.append((wo_hbm.at[piece], wo_ref.at[piece]))
     loads = [
         pltpu.make_async_copy(src, dst, local_sems.at[i]) for i, (src, dst) in enumerate(pairs)
     ]
     for load in loads:
         load.start()
 
+    def descriptor(src, dst, sems, peer, owner):
+        return pltpu.make_async_remote_copy(
+            src_ref=src(peer),
+            dst_ref=dst(owner),
+            send_sem=sems.at[0, peer],
+            recv_sem=sems.at[1, owner],
+            device_id={"gx": peer},
+            device_id_type=MESH,
+        )
+
     def exchange(src, dst, sems):
-        copies = [
-            pltpu.make_async_remote_copy(
-                src_ref=src(peer),
-                dst_ref=dst.at[me],
-                send_sem=sems.at[0, peer],
-                recv_sem=sems.at[1, me],
-                device_id={"gx": peer},
-                device_id_type=MESH,
-            )
-            for peer in peers
-        ]
+        copies = [descriptor(src, dst, sems, peer, me) for peer in peers]
         for copy in copies:
             copy.start()
         return copies
 
     def arrive(src, dst, sems):
         for peer in peers:
-            pltpu.make_async_remote_copy(
-                src_ref=src(peer),
-                dst_ref=dst.at[peer],
-                send_sem=sems.at[0, peer],
-                recv_sem=sems.at[1, peer],
-                device_id={"gx": peer},
-                device_id_type=MESH,
-            ).wait_recv()
+            descriptor(src, dst, sems, peer, peer).wait_recv()
 
     row = hidden_ref[...].astype(jnp.float32)
     inv_row = lax.rsqrt(jnp.mean(row * row, axis=-1, keepdims=True) + 1e-05)
@@ -113,13 +106,14 @@
         x_send[j, :, cols:] = inv_lanes
     x_recv[me] = x_send[me]
     pl.semaphore_wait(barrier, gx)
-    x_copies = exchange(lambda peer: x_send.at[peer], x_recv, x_sems)
+    x_route = (lambda peer: x_send.at[peer], lambda peer: x_recv.at[peer], x_sems)
+    copies = exchange(*x_route)
 
     half = head // 2
     lane = lax.broadcasted_iota(jnp.int32, (1, head), 1)
     index = jnp.where(lane < half, lane, lane - half).astype(jnp.float32)
     freqs = jnp.exp(-math.log(500000.0) * (index * (2.0 / head)))
-    length = length_ref[0]
+    length = ints_ref[:, 1:]
     angles = length.astype(jnp.float32) * freqs
     cosine = jnp.cos(angles)
     sine = jnp.sin(angles)
@@ -127,10 +121,10 @@
 
     loads[0].wait()
     table = gains_ref[...].astype(jnp.float32)
-    chosen = lax.broadcasted_iota(jnp.int32, table.shape, 0) == layer_ref[0]
+    chosen = lax.broadcasted_iota(jnp.int32, table.shape, 0) == ints_ref[:, :1]
     gain = jnp.sum(jnp.where(chosen, table, 0.0), axis=0, keepdims=True)
 
-    arrive(lambda peer: x_send.at[peer], x_recv, x_sems)
+    arrive(*x_route)
     x32 = x_recv[:, 0, :cols]
     inv = x_recv[:, 0, cols : cols + 1]
     normed = (x32 * inv * gain).astype(jnp.bfloat16)
@@ -140,30 +134,49 @@
         for h in range(sums.shape[1] // head):
             p_send[:, first + h, :] = sums[:, h * head : (h + 1) * head]
 
-    for i in range(QUERY_PIECES):
-        loads[1 + i].wait()
-        project(wq_ref[:, i * width : (i + 1) * width], i * width // head)
-    loads[1 + QUERY_PIECES].wait()
-    project(wk_ref[...], q_local)
-    loads[2 + QUERY_PIECES].wait()
-    project(wv_ref[...], q_local + kv_local)
-    p_copies = exchange(lambda peer: p_send.at[peer], p_recv, p_sems)
+    def p_route(first, count, sems):
+        rows = pl.ds(first, count)
+        return lambda peer: p_send.at[peer, rows], lambda peer: p_recv.at[peer, rows], sems
+
+    def summed_rows(first, count):
+        rows = slice(first, first + count)
+        total = p_recv[0, rows]
+        for j in range(1, gx):
+            total = total + p_recv[j, rows]
+        return total
+
+    def turn(total):
+        return total * cosine + pltpu.roll(total, half, 1) * sine
+
+    early = 2 * kv_local + group
+    late = (kv_local - 1) * group
+    early_route = p_route(0, early, p_sems.at[0])
+    late_route = p_route(early, late, p_sems.at[1])
+    loads[1].wait()
+    project(wk_ref[...], 0)
+    loads[2].wait()
+    project(wv_ref[...], kv_local)
+    loads[3].wait()
+    project(wq_ref[:, :width], 2 * kv_local)
+    copies += exchange(*early_route)
+    for i in range(1, kv_local):
+        loads[3 + i].wait()
+        project(wq_ref[:, i * width : (i + 1) * width], 2 * kv_local + i * group)
+    copies += exchange(*late_route)
     p_recv[me] = p_send[me]
-    loads[3 + QUERY_PIECES].wait()
-    loads[4 + QUERY_PIECES].wait()
-    arrive(lambda peer: p_send.at[peer], p_recv, p_sems)
-    total = p_recv[0]
-    for j in range(1, gx):
-        total = total + p_recv[j]
-
-    rotated = total * cosine + pltpu.roll(total, half, 1) * sine
+    loads[3 + kv_local].wait()
+    loads[4 + kv_local].wait()
+    arrive(*early_route)
+    fresh = summed_rows(0, early)
+    turned = turn(fresh)
+
     scale = 1.0 / math.sqrt(head)
     valid = lax.broadcasted_iota(jnp.int32, (1, slots), 1) < length
-    for g in range(kv_local):
-        rq = rotated[g * group : (g + 1) * group].astype(jnp.bfloat16)
-        rk = rotated[q_local + g : q_local + g + 1].astype(jnp.bfloat16).astype(jnp.float32)
-        first = q_local + kv_local + g
-        nv = total[first : first + 1].astype(jnp.bfloat16).astype(jnp.float32)
+
+    def attend(g, rotated):
+        rq = rotated.astype(jnp.bfloat16)
+        rk = turned[g : g + 1].astype(jnp.bfloat16).astype(jnp.float32)
+        nv = fresh[kv_local + g : kv_local + g + 1].astype(jnp.bfloat16).astype(jnp.float32)
         scores = (
             lax.dot_general(
                 rq, kc_ref[g], (((1,), (1,)), ((), ())), preferred_element_type=jnp.float32
@@ -178,20 +191,46 @@
         denominator = jnp.sum(exps, axis=-1, keepdims=True) + own_exp
         probs = (exps / denominator).astype(jnp.bfloat16)
         own_prob = (own_exp / denominator).astype(jnp.bfloat16).astype(jnp.float32)
-        attn = jnp.dot(probs, vc_ref[g], preferred_element_type=jnp.float32) + own_prob * nv
-        a_send[g * group : (g + 1) * group, :] = attn.astype(jnp.bfloat16).astype(jnp.float32)
-    a_copies = exchange(lambda peer: a_send, a_recv, a_sems)
-    a_recv[me] = a_send[...]
+        return jnp.dot(probs, vc_ref[g], preferred_element_type=jnp.float32) + own_prob * nv
+
+    attn = [attend(0, turned[2 * kv_local :])]
+    arrive(*late_route)
+    queries = turn(summed_rows(early, late))
+    span = q_local // OUT_PIECES
+    groups = kv_local // OUT_PIECES
+    a_routes = []
     for i in range(OUT_PIECES):
-        loads[5 + QUERY_PIECES + i].wait()
-    arrive(lambda peer: a_send, a_recv, a_sems)
-    attended = jnp.concatenate([a_recv[:, h, :] for h in range(q_local)], axis=1).astype(
-        jnp.bfloat16
-    )
+        while len(attn) < (i + 1) * groups:
+            g = len(attn)
+            attn.append(attend(g, queries[(g - 1) * group : g * group]))
+        piece = jnp.concatenate(attn[i * groups : (i + 1) * groups], axis=0)
+        piece = piece.astype(jnp.bfloat16)
+        a_send[i] = piece
+        route = (
+            lambda peer, i=i: a_send.at[i],
+            lambda peer, i=i: a_recv.at[i, peer],
+            a_sems.at[i],
+        )
+        copies += exchange(*route)
+        a_recv[i, me] = piece
+        a_routes.append(route)
+    out_width = wo_ref.shape[1] // OUT_PIECES
+    total = None
+    for i in range(OUT_PIECES):
+        loads[5 + kv_local + i].wait()
+        arrive(*a_routes[i])
+        a_wide[i] = a_recv[i].astype(jnp.float32)
+        attended = jnp.concatenate([a_wide[i, :, h, :] for h in range(span)], axis=1)
+        attended = attended.astype(jnp.bfloat16)
+        rows = slice(i * depth, (i + 1) * depth)
+        if i < OUT_PIECES - 1:
+            term = jnp.dot(attended, wo_ref[rows], preferred_element_type=jnp.float32)
+            total = term if total is None else total + term
     y_copies = []
     for i in range(OUT_PIECES):
         piece = slice(i * out_width, (i + 1) * out_width)
-        y_send[i] = jnp.dot(attended, wo_ref[:, piece], preferred_element_type=jnp.float32)
+        term = jnp.dot(attended, wo_ref[rows, piece], preferred_element_type=jnp.float32)
+        y_send[i] = total[:, piece] + term
         copy = pltpu.make_async_remote_copy(
             src_ref=y_send.at[i],
             dst_ref=y_recv.at[i],
@@ -207,7 +246,7 @@
         piece = slice(i * out_width, (i + 1) * out_width)
         summed = y_send[i] + y_recv[i]
         out_ref[:, piece] = (x_recv[:, 0, piece] + summed).astype(out_ref.dtype)
-    for copy in x_copies + p_copies + a_copies + y_copies:
+    for copy in copies + y_copies:
         copy.wait_send()
 
 
@@ -230,14 +269,13 @@
     heads = q_local + 2 * kv_local
     f32, bf16 = jnp.float32, jnp.bfloat16
     vmem = pl.BlockSpec(memory_space=pltpu.VMEM)
-    smem = pl.BlockSpec(memory_space=pltpu.SMEM)
     anywhere = pl.BlockSpec(memory_space=pl.ANY)
     dma = pltpu.SemaphoreType.DMA
     weights = w_query.size + key_weight.size + value_weight.size + w_out.size
     return pl.pallas_call(
         functools.partial(kernel, gx),
         out_shape=jax.ShapeDtypeStruct((gx, cols), bf16),
-        in_specs=[vmem, smem, smem] + [anywhere] * 7,
+        in_specs=[vmem, vmem] + [anywhere] * 7,
         out_specs=vmem,
         scratch_shapes=[
             pltpu.VMEM(norm_gains.shape, bf16),
@@ -251,14 +289,15 @@
             pltpu.VMEM((gx, 1, cols + LANES), f32),
             pltpu.VMEM((gx, heads, head), f32),
             pltpu.VMEM((gx, heads, head), f32),
-            pltpu.VMEM((q_local, head), f32),
-            pltpu.VMEM((gx, q_local, head), f32),
+            pltpu.VMEM((OUT_PIECES, q_local // OUT_PIECES, head), bf16),
+            pltpu.VMEM((OUT_PIECES, gx, q_local // OUT_PIECES, head), bf16),
+            pltpu.VMEM((OUT_PIECES, gx, q_local // OUT_PIECES, head), f32),
             pltpu.VMEM((OUT_PIECES, gx, cols // OUT_PIECES), f32),
             pltpu.VMEM((OUT_PIECES, gx, cols // OUT_PIECES), f32),
-            dma((5 + QUERY_PIECES + OUT_PIECES,)),
+            dma((5 + kv_local + OUT_PIECES,)),
             dma((2, gx)),
-            dma((2, gx)),
-            dma((2, gx)),
+            dma((2, 2, gx)),
+            dma((OUT_PIECES, 2, gx)),
             dma((2, OUT_PIECES)),
         ],
         compiler_params=pltpu.CompilerParams(
@@ -269,8 +308,7 @@
         ),
     )(
         hidden,
-        exit_layer,
-        lengths,
+        jnp.concatenate([exit_layer, lengths])[None, :],
         norm_gains,
         w_query,
         key_weight,

time: 28.7 us -> 28 us (0.976)
  Pallas kernels: 25.8 us -> 24.5 us
  other arithmetic: 0 us -> 0.59 us
    pallas_call x1, Pallas kernels: 25.8 us -> 24.5 us  [fused(): pl.pallas_call(functools.partial(kernel, gx), out_shape=jax.ShapeDtypeStr...]
    broadcast_in_dim x0 -> x1, other arithmetic: none -> 0.59 us  [fused(): jnp.concatenate([exit_layer, lengths])[None, :]]
where the time goes in v2:
time: 28 us; the launch traced here: 27.7 us
  Pallas kernels  24.5 us (88%)
  local copies, waits for them, and re-layouts  1.32 us (5%)
  between operations  1.31 us (5%)
  other arithmetic  0.59 us (2%)
    pallas_call x1, Pallas kernels, fused(): pl.pallas_call(functools.partial(kernel, gx), out_shape=jax.ShapeDtypeStr...  24.5 us
    unnamed x1, local copies, waits for them, and re-layouts  1.32 us
    broadcast_in_dim x1, other arithmetic, fused(): jnp.concatenate([exit_layer, lengths])[None, :]  0.59 us

profile of v2, /device:TPU:0, one launch (start us, length us, event | category | flops | bytes accessed | tf_op | source)
XLA Modules:
  0.0 27.7 jit_solution(18166534230074859892)
XLA Ops:
  1.3 0.6 %add_bitcast_fusion.ints_ref = s32[1,2]{1,0:T(1,128)} fusion(s32[1]{0:T(128)S(6)} %copy.13, s32[1]{0:T(128)S(6)} %copy.12), kind=kLoop, calls=%fused_computation | loop fusion | flops 2 | bytes 16 | tf_op jit(solution)/shard_map/broadcast_in_dim | solution.py:311
  1.9 24.5 %shard_map.100 = bf16[8,1024]{1,0:T(8,128)(2,1)} custom-call(bf16[1,8192]{1,0:T(2,128)(2,1)} %hidden_ref.1, s32[1,2]{1,0:T(1,128)} %add_bitcast_fusion.ints_ref, bf16[80,1024]{1,0:T(8,128)(2,1)} %gains_hbm.1, bf16[1024,4096]{1,0:T(8,128)(2,1)} %wq_hbm.1, bf16[1024,512]{1,0:T(8,128)(2,1)} %wk_hbm.1, bf16[1024,512]{1,0:T(8,128)(2,1)} %wv_hbm.1, ...), custom_call_target="tpu_custom_call" | custom-call | flops 150994944 | bytes 18874368 | tf_op jit(solution)/shard_map/pallas_call | solution.py:275
  26.4 1.3 %copy.14 = bf16[8,1024]{1,0:T(8,128)(2,1)} copy(bf16[8,1024]{1,0:T(8,128)(2,1)} %shard_map.100) | data formatting | bytes 32768

commit v3 on v2

--- a/solution.py
+++ b/solution.py
@@ -16,7 +16,8 @@
 def kernel(
     gx,
     hidden_ref,
-    ints_ref,
+    layer_hbm,
+    length_hbm,
     gains_hbm,
     wq_hbm,
     wk_hbm,
@@ -25,6 +26,8 @@
     kc_hbm,
     vc_hbm,
     out_ref,
+    layer_ref,
+    length_ref,
     gains_ref,
     wq_ref,
     wk_ref,
@@ -63,7 +66,7 @@
 
     width = wq_ref.shape[1] // kv_local
     depth = wo_ref.shape[0] // OUT_PIECES
-    pairs = [(gains_hbm, gains_ref)]
+    pairs = [(layer_hbm, layer_ref), (length_hbm, length_ref), (gains_hbm, gains_ref)]
     pairs += [(wk_hbm, wk_ref), (wv_hbm, wv_ref)]
     for i in range(kv_local):
         piece = pl.ds(i * width, width)
@@ -113,15 +116,17 @@
     lane = lax.broadcasted_iota(jnp.int32, (1, head), 1)
     index = jnp.where(lane < half, lane, lane - half).astype(jnp.float32)
     freqs = jnp.exp(-math.log(500000.0) * (index * (2.0 / head)))
-    length = ints_ref[:, 1:]
+    loads[1].wait()
+    length = length_ref[0]
     angles = length.astype(jnp.float32) * freqs
     cosine = jnp.cos(angles)
     sine = jnp.sin(angles)
     sine = jnp.where(lane < half, -sine, sine)
 
     loads[0].wait()
+    loads[2].wait()
     table = gains_ref[...].astype(jnp.float32)
-    chosen = lax.broadcasted_iota(jnp.int32, table.shape, 0) == ints_ref[:, :1]
+    chosen = lax.broadcasted_iota(jnp.int32, table.shape, 0) == layer_ref[0]
     gain = jnp.sum(jnp.where(chosen, table, 0.0), axis=0, keepdims=True)
 
     arrive(*x_route)
@@ -152,20 +157,20 @@
     late = (kv_local - 1) * group
     early_route = p_route(0, early, p_sems.at[0])
     late_route = p_route(early, late, p_sems.at[1])
-    loads[1].wait()
+    loads[3].wait()
     project(wk_ref[...], 0)
-    loads[2].wait()
+    loads[4].wait()
     project(wv_ref[...], kv_local)
-    loads[3].wait()
+    loads[5].wait()
     project(wq_ref[:, :width], 2 * kv_local)
     copies += exchange(*early_route)
     for i in range(1, kv_local):
-        loads[3 + i].wait()
+        loads[5 + i].wait()
         project(wq_ref[:, i * width : (i + 1) * width], 2 * kv_local + i * group)
     copies += exchange(*late_route)
     p_recv[me] = p_send[me]
-    loads[3 + kv_local].wait()
-    loads[4 + kv_local].wait()
+    loads[5 + kv_local].wait()
+    loads[6 + kv_local].wait()
     arrive(*early_route)
     fresh = summed_rows(0, early)
     turned = turn(fresh)
@@ -217,7 +222,7 @@
     out_width = wo_ref.shape[1] // OUT_PIECES
     total = None
     for i in range(OUT_PIECES):
-        loads[5 + kv_local + i].wait()
+        loads[7 + kv_local + i].wait()
         arrive(*a_routes[i])
         a_wide[i] = a_recv[i].astype(jnp.float32)
         attended = jnp.concatenate([a_wide[i, :, h, :] for h in range(span)], axis=1)
@@ -269,15 +274,18 @@
     heads = q_local + 2 * kv_local
     f32, bf16 = jnp.float32, jnp.bfloat16
     vmem = pl.BlockSpec(memory_space=pltpu.VMEM)
+    hbm = pl.BlockSpec(memory_space=pltpu.HBM)
     anywhere = pl.BlockSpec(memory_space=pl.ANY)
     dma = pltpu.SemaphoreType.DMA
     weights = w_query.size + key_weight.size + value_weight.size + w_out.size
     return pl.pallas_call(
         functools.partial(kernel, gx),
         out_shape=jax.ShapeDtypeStruct((gx, cols), bf16),
-        in_specs=[vmem, vmem] + [anywhere] * 7,
+        in_specs=[vmem, hbm, hbm] + [anywhere] * 7,
         out_specs=vmem,
         scratch_shapes=[
+            pltpu.SMEM(exit_layer.shape, jnp.int32),
+            pltpu.SMEM(lengths.shape, jnp.int32),
             pltpu.VMEM(norm_gains.shape, bf16),
             pltpu.VMEM(w_query.shape, bf16),
             pltpu.VMEM(key_weight.shape, bf16),
@@ -294,7 +302,7 @@
             pltpu.VMEM((OUT_PIECES, gx, q_local // OUT_PIECES, head), f32),
             pltpu.VMEM((OUT_PIECES, gx, cols // OUT_PIECES), f32),
             pltpu.VMEM((OUT_PIECES, gx, cols // OUT_PIECES), f32),
-            dma((5 + kv_local + OUT_PIECES,)),
+            dma((7 + kv_local + OUT_PIECES,)),
             dma((2, gx)),
             dma((2, 2, gx)),
             dma((OUT_PIECES, 2, gx)),
@@ -308,7 +316,8 @@
         ),
     )(
         hidden,
-        jnp.concatenate([exit_layer, lengths])[None, :],
+        exit_layer,
+        lengths,
         norm_gains,
         w_query,
         key_weight,

time: 28 us -> 27.4 us (0.979)
  other arithmetic: 0.59 us -> 0 us
    broadcast_in_dim x1 -> x0, other arithmetic: 0.59 us -> none  [fused(): jnp.concatenate([exit_layer, lengths])[None, :]]
where the time goes in v3:
time: 27.4 us; the launch traced here: 27.2 us
  Pallas kernels  24.6 us (90%)
  local copies, waits for them, and re-layouts  1.32 us (5%)
  between operations  1.3 us (5%)
    pallas_call x1, Pallas kernels, fused(): pl.pallas_call(functools.partial(kernel, gx), out_shape=jax.ShapeDtypeStr...  24.6 us
    unnamed x1, local copies, waits for them, and re-layouts  1.32 us

profile of v3, /device:TPU:0, one launch (start us, length us, event | category | flops | bytes accessed | tf_op | source)
XLA Modules:
  0.0 27.2 jit_solution(4360945785657527608)
XLA Ops:
  1.3 24.6 %shard_map.100 = bf16[8,1024]{1,0:T(8,128)(2,1)} custom-call(bf16[1,8192]{1,0:T(2,128)(2,1)} %hidden_ref.1, s32[1]{0:T(128)S(6)} %copy.12.layer_hbm, s32[1]{0:T(128)S(6)} %copy.13.length_hbm, bf16[80,1024]{1,0:T(8,128)(2,1)} %gains_hbm.1, bf16[1024,4096]{1,0:T(8,128)(2,1)} %wq_hbm.1, bf16[1024,512]{1,0:T(8,128)(2,1)} %wk_hbm.1, bf16[1024,512]{1,0:T(8,128)(2,1)} %wv_hbm.1, ...), custom_call_target="tpu_custom_call" | custom-call | flops 150994944 | bytes 18874368 | tf_op jit(solution)/shard_map/pallas_call | solution.py:281
  25.9 1.3 %copy.14 = bf16[8,1024]{1,0:T(8,128)(2,1)} copy(bf16[8,1024]{1,0:T(8,128)(2,1)} %shard_map.100) | data formatting | bytes 32768

commit v4 on v3

--- a/solution.py
+++ b/solution.py
@@ -78,7 +78,7 @@
     loads = [
         pltpu.make_async_copy(src, dst, local_sems.at[i]) for i, (src, dst) in enumerate(pairs)
     ]
-    for load in loads:
+    for load in loads[: 5 + kv_local]:
         load.start()
 
     def descriptor(src, dst, sems, peer, owner):
@@ -111,6 +111,8 @@
     pl.semaphore_wait(barrier, gx)
     x_route = (lambda peer: x_send.at[peer], lambda peer: x_recv.at[peer], x_sems)
     copies = exchange(*x_route)
+    for load in loads[5 + kv_local :]:
+        load.start()
 
     half = head // 2
     lane = lax.broadcasted_iota(jnp.int32, (1, head), 1)

time: 27.4 us -> 27.4 us (level)
  no operation moved by 1% of the time
where the time goes in v4:
time: 27.4 us; the launch traced here: 27.2 us
  Pallas kernels  24.6 us (90%)
  local copies, waits for them, and re-layouts  1.32 us (5%)
  between operations  1.3 us (5%)
    pallas_call x1, Pallas kernels, fused(): pl.pallas_call(functools.partial(kernel, gx), out_shape=jax.ShapeDtypeStr...  24.6 us
    unnamed x1, local copies, waits for them, and re-layouts  1.32 us

profile of v4, /device:TPU:0, one launch (start us, length us, event | category | flops | bytes accessed | tf_op | source)
XLA Modules:
  0.0 27.2 jit_solution(2878568180584479483)
XLA Ops:
  1.3 24.6 %shard_map.100 = bf16[8,1024]{1,0:T(8,128)(2,1)} custom-call(bf16[1,8192]{1,0:T(2,128)(2,1)} %hidden_ref.1, s32[1]{0:T(128)S(6)} %copy.12.layer_hbm, s32[1]{0:T(128)S(6)} %copy.13.length_hbm, bf16[80,1024]{1,0:T(8,128)(2,1)} %gains_hbm.1, bf16[1024,4096]{1,0:T(8,128)(2,1)} %wq_hbm.1, bf16[1024,512]{1,0:T(8,128)(2,1)} %wk_hbm.1, bf16[1024,512]{1,0:T(8,128)(2,1)} %wv_hbm.1, ...), custom_call_target="tpu_custom_call" | custom-call | flops 150994944 | bytes 18874368 | tf_op jit(solution)/shard_map/pallas_call | solution.py:283
  25.9 1.3 %copy.14 = bf16[8,1024]{1,0:T(8,128)(2,1)} copy(bf16[8,1024]{1,0:T(8,128)(2,1)} %shard_map.100) | data formatting | bytes 32768
